TPU v7x, 32 devices: a whole 2x2x4 slice. The times are simulated.
32 devices in a mesh: groups: 2 (over y), blk: 4 (over z), rhs: 2 (over x), sub: 2 (over core).
Axes of the slice: x: 2, y: 2, z: 4, core: 2. Of those that a mesh axis runs over, the one named last changes fastest.
Arguments:
- coords: bfloat16 [64, 16384], P(None, ('groups', 'blk')), parts along dimension 1, may hold values from -1.5 to 1.5
- values: bfloat16 [64, 16384], P('rhs', ('groups', 'blk')), parts along dimension 1, may hold values from -6 to 6
- tree_order: int32 [16384], P(('groups', 'blk')), parts along dimension 0, may hold values from 0 to 8191, as said below
- near_mask: int32 [8, 2], P(('groups', 'blk')), parts along dimension 0, may hold values 0 or 1
- skel_leaf: int32 [8, 256], P(('groups', 'blk')), parts along dimension 0, may hold values from 0 to 2047, as said below
- skel_up: int32 [4, 256], P('groups'), parts along dimension 0, may hold values from 0 to 511, as said below
Outputs:
- product: float32 [64, 8, 2048], P('rhs', ('groups', 'blk'), 'sub'), parts along dimension 1
There are 2 independent parts, one for each index of `groups`. A program takes and returns all parts, laid end to end along the dimension named above; each array names one. Nothing has to cross between parts.
Inputs may be any that keep to these rules, and one draw needn't show every extreme that they name: Each sample appears once, and position p and sample tree_order[p] lie in the same span of 2048 positions. `skel_leaf`: each row holds 256 different row numbers within its leaf. `skel_up`: each row holds 256 different positions among the 512 skeleton samples of the node's two children, the left child's first.
All inputs are finite; a program needn't handle non-finite values. No bound on the sum of `near_mask` on one device may be relied on, other than what follows from the above.
Results may differ from a plain program's by a relative error of at most 0.00075.
Values may be sent and summed in bfloat16 or wider, within the bound.
A program may use at most 64 MiB of HBM per device.

v0:
```python
import functools

import jax
import jax.numpy as jnp
from jax import lax
from jax.experimental import pallas as pl
from jax.experimental.pallas import tpu as pltpu
from jax.sharding import PartitionSpec as P

MESH = pl.DeviceIdType.MESH
DEPTH = 128
CHUNK = 256


def norm_rows(x, is_source, features):
    wide = x.astype(jnp.float32)
    norm = (-32.0 / features) * jnp.sum(wide * wide, axis=0, keepdims=True)
    high = norm.astype(jnp.bfloat16).astype(jnp.float32)
    rest = norm - high
    middle = rest.astype(jnp.bfloat16).astype(jnp.float32)
    low = rest - middle
    row = lax.broadcasted_iota(jnp.int32, (16, x.shape[1]), 0)
    first = 0 if is_source else 3
    ones = (row >= 3 - first) & (row < 6 - first)
    rows = jnp.where(ones, 1.0, 0.0)
    for place, part in enumerate((high, middle, low)):
        rows = jnp.where(row == first + place, part, rows)
    return rows.astype(jnp.bfloat16)


def augmented(x, is_source):
    features, count = x.shape
    scaled = x if is_source else (x.astype(jnp.float32) * (64.0 / features)).astype(jnp.bfloat16)
    pad = jnp.zeros((DEPTH - features - 16, count), jnp.bfloat16)
    return jnp.concatenate([scaled, norm_rows(x, is_source, features), pad], axis=0)


def one_hot(count, first, index):
    row = lax.broadcasted_iota(jnp.int32, (count, index.shape[1]), 0) + first
    return jnp.where(row == index, 1.0, 0.0).astype(jnp.bfloat16)


def dot(left, right):
    return jnp.dot(left, right, preferred_element_type=jnp.float32)


def body(
    sizes,
    coords,
    values,
    order,
    mask,
    skel,
    skel_up,
    out,
    xs,
    vs,
    packs,
    sibs,
    src_t,
    scaled,
    tgt,
    z_send,
    z_recv,
    f_send,
    f_recv,
    p_send,
    p_recv,
):
    blk_size, sub_size = sizes
    features, rows = coords.shape
    skeleton = skel.shape[1]
    half = rows // sub_size
    bits = blk_size.bit_length() - 1
    total_leaves = skel_up.shape[0] + 2
    blk = lax.axis_index("blk")
    rhs = lax.axis_index("rhs")
    sub = lax.axis_index("sub")

    def flip(number, bit):
        return number + bit - 2 * bit * ((number // bit) % 2)

    across = flip(rhs, 1)
    other = 1 - sub
    near_1, near_2 = {"blk": flip(blk, 1)}, {"blk": flip(blk, 2)}
    chip_mates = [{"rhs": across}, {"sub": other}, {"rhs": across, "sub": other}]
    partners = [near_1, near_2] + chip_mates
    partners += [{"blk": flip(blk, 2**bit)} for bit in range(2, bits)]

    barrier = pltpu.get_barrier_semaphore()
    for partner in partners:
        pl.semaphore_signal(barrier, inc=1, device_id=partner, device_id_type=MESH)
    pl.semaphore_wait(barrier, len(partners))

    share = features // 4
    quarter = pl.ds(pl.multiple_of((sub * 2 + rhs % 2) * share, share), share)
    lanes = pl.ds(pl.multiple_of(sub * half, half), half)

    def remote(source, target, send, recv, partner):
        return pltpu.make_async_remote_copy(
            src_ref=source,
            dst_ref=target,
            send_sem=send,
            recv_sem=recv,
            device_id=partner,
            device_id_type=MESH,
        )

    def far_copies(slot, from_x, from_v, partner):
        return [
            remote(from_x.at[quarter], xs.at[slot, quarter], z_send.at[slot, 0], z_recv.at[slot, 0], partner),
            remote(
                from_v.at[:, lanes], vs.at[slot, :, lanes], z_send.at[slot, 1], z_recv.at[slot, 1], partner
            ),
        ]

    hops = [far_copies(0, coords, values, near_1), far_copies(1, coords, values, near_2)]
    hops.append(far_copies(2, xs.at[1], vs.at[1], near_1))

    def spread_copies(slot):
        found = [
            remote(
                xs.at[slot, quarter],
                xs.at[slot, quarter],
                f_send.at[slot, place],
                f_recv.at[slot, place],
                mate,
            )
            for place, mate in enumerate(chip_mates)
        ]
        block = vs.at[slot, :, lanes]
        found.append(remote(block, block, f_send.at[slot, 3], f_recv.at[slot, 3], chip_mates[1]))
        return found

    spreads = [spread_copies(slot) for slot in range(3)]
    pack_copies = [
        remote(packs.at[bit], sibs.at[bit], p_send.at[bit], p_recv.at[bit], {"blk": flip(blk, 2**bit)})
        for bit in range(bits)
    ]

    def start(copies):
        for copy in copies:
            copy.start()

    def arrive(copies):
        for copy in copies:
            copy.wait_recv()

    start(hops[0])
    start(hops[1])

    local = order[...] - blk * rows
    own = coords[...]
    mine = order[:, lanes] - blk * rows
    skel_hot = one_hot(rows, 0, skel[...])
    digits = jnp.concatenate([local // 256, local % 256], axis=0).astype(jnp.float32)
    digits = jnp.concatenate([digits, jnp.zeros((14, rows), jnp.float32)], axis=0).astype(jnp.bfloat16)
    places = dot(digits, skel_hot)
    skel_rows = (places[0:1] * 256.0 + places[1:2]).astype(jnp.int32)
    src_t[0] = augmented(own, True).T

    def gathered(pieces, index):
        total = None
        for piece, first in pieces:
            term = dot(piece, one_hot(piece.shape[1], first, index))
            total = term if total is None else total + term
        return total.astype(jnp.bfloat16)

    pieces = [(own[:, first : first + 512], first) for first in range(0, rows, 512)]
    z = gathered(pieces, skel_rows)
    z_tgt = augmented(z, False)
    total = jnp.zeros((values.shape[0], skeleton), jnp.float32)
    for first in range(0, rows, 512):
        tile = jnp.exp(dot(src_t[0, first : first + 512], z_tgt)).astype(jnp.bfloat16)
        total = total + dot(values[:, first : first + 512], tile)
    packs[0, :features] = z
    packs[0, features:] = total.astype(jnp.bfloat16)
    pack_copies[0].start()
    tgt[...] = augmented(gathered(pieces, mine), False)

    arrive(hops[0])
    start(spreads[0])

    out[...] = jnp.zeros_like(out)

    def near(slot, weights):
        def step(index, carry):
            at = pl.ds(pl.multiple_of(index * CHUNK, CHUNK), CHUNK)
            tile = jnp.exp(dot(src_t[slot, at], tgt[...])).astype(jnp.bfloat16)
            out[...] += dot(weights[:, at], tile)
            return carry

        lax.fori_loop(0, rows // CHUNK, step, 0)

    near(0, values)

    arrive(hops[1])
    start(hops[2])
    start(spreads[1])

    def near_slot(slot, column):
        arrive(spreads[slot])
        src_t[slot + 1] = augmented(xs[slot], True).T
        factor = mask[0, column].astype(jnp.float32)
        scaled[slot] = (vs[slot].astype(jnp.float32) * factor).astype(jnp.bfloat16)
        near(slot + 1, scaled.at[slot])

    def merge(bit):
        on_right = (blk // 2**bit) % 2
        first_row = total_leaves - (total_leaves >> bit) + blk // 2 ** (bit + 1)
        chosen = skel_up[pl.ds(first_row, 1)]
        pack_copies[bit].wait_recv()
        mine_z, other_z = packs[bit, :features], sibs[bit, :features]
        parent = gathered(
            [(mine_z, on_right * skeleton), (other_z, (1 - on_right) * skeleton)], chosen
        )
        parent_tgt = augmented(parent, False)
        summed = None
        for pack, side in ((packs, mine_z), (sibs, other_z)):
            tile = jnp.exp(dot(augmented(side, True).T, parent_tgt)).astype(jnp.bfloat16)
            term = dot(pack[bit, features:], tile)
            summed = term if summed is None else summed + term
        packs[bit + 1, :features] = parent
        packs[bit + 1, features:] = summed.astype(jnp.bfloat16)
        pack_copies[bit + 1].start()

    near_slot(0, 0)
    merge(0)
    arrive(hops[2])
    start(spreads[2])
    near_slot(1, 1)
    for bit in range(1, bits - 1):
        merge(bit)
    near_slot(2, 1)
    pack_copies[bits - 1].wait_recv()
    for bit in range(bits):
        weights = sibs[bit, features:]
        if bit < 2:
            factor = (1 - mask[0, bit]).astype(jnp.float32)
            weights = (weights.astype(jnp.float32) * factor).astype(jnp.bfloat16)
        tile = jnp.exp(dot(augmented(sibs[bit, :features], True).T, tgt[...])).astype(jnp.bfloat16)
        out[...] += dot(weights, tile)

    for copies in hops + spreads + [pack_copies]:
        for copy in copies:
            copy.wait_send()


def shards(mesh, coords, values, tree_order, near_mask, skel_leaf, skel_up):
    features, rows = coords.shape
    columns = values.shape[0]
    skeleton = skel_leaf.shape[1]
    sub_size = mesh.shape["sub"]
    bits = mesh.shape["blk"].bit_length() - 1
    half = rows // sub_size
    held = max(columns, 16)
    if held > columns:
        values = jnp.pad(values, ((0, held - columns), (0, 0)))
    vmem = pl.BlockSpec(memory_space=pltpu.VMEM)
    result = pl.pallas_call(
        functools.partial(body, (mesh.shape["blk"], sub_size)),
        out_shape=jax.ShapeDtypeStruct((held, half), jnp.float32),
        in_specs=[vmem, vmem, vmem, pl.BlockSpec(memory_space=pltpu.SMEM), vmem, vmem],
        out_specs=vmem,
        scratch_shapes=[
            pltpu.VMEM((3, features, rows), jnp.bfloat16),
            pltpu.VMEM((3, held, rows), jnp.bfloat16),
            pltpu.VMEM((bits, features + held, skeleton), jnp.bfloat16),
            pltpu.VMEM((bits, features + held, skeleton), jnp.bfloat16),
            pltpu.VMEM((4, rows, DEPTH), jnp.bfloat16),
            pltpu.VMEM((3, held, rows), jnp.bfloat16),
            pltpu.VMEM((DEPTH, half), jnp.bfloat16),
            pltpu.SemaphoreType.DMA((3, 2)),
            pltpu.SemaphoreType.DMA((3, 2)),
            pltpu.SemaphoreType.DMA((3, 4)),
            pltpu.SemaphoreType.DMA((3, 4)),
            pltpu.SemaphoreType.DMA((bits,)),
            pltpu.SemaphoreType.DMA((bits,)),
        ],
        compiler_params=pltpu.CompilerParams(
            collective_id=0, has_side_effects=True, vmem_limit_bytes=48 * 2**20
        ),
    )(coords, values, tree_order.reshape(1, rows), near_mask, skel_leaf, skel_up)
    return result[:columns].reshape(columns, 1, half)


def solution(mesh):
    return jax.shard_map(
        functools.partial(shards, mesh),
        mesh=mesh,
        in_specs=(
            P(None, ("groups", "blk")),
            P("rhs", ("groups", "blk")),
            P(("groups", "blk")),
            P(("groups", "blk"), None),
            P(("groups", "blk"), None),
            P("groups", None),
        ),
        out_specs=P("rhs", ("groups", "blk"), "sub"),
        check_vma=False,
    )
```

profile of v0, /device:TPU:0, one launch (start us, length us, event | category | flops | bytes accessed | tf_op | source)
XLA Modules:
  0.0 35.2 jit_solution(18408629466593023013)
XLA Ops:
  0.0 0.0 copy-start.4
  0.0 0.0 copy-start.5
  0.0 0.7 %copy-done.4 = s32[1,256]{1,0:T(1,128)S(1)} copy-done((s32[1,256]{1,0:T(1,128)S(1)}, s32[1,256]{1,0:T(1,128)}, u32[]{:S(2)}) %copy-start.4) | copy-done | bytes 1048
  0.7 0.0 copy-done.5
  0.7 0.0 copy-start
  0.7 0.9 %copy-done = bf16[64,2048]{1,0:T(8,128)(2,1)S(1)} copy-done((bf16[64,2048]{1,0:T(8,128)(2,1)S(1)}, bf16[64,2048]{1,0:T(8,128)(2,1)}, u32[]{:S(2)}) %copy-start) | copy-done | bytes 262168
  1.6 0.0 copy-start.1
  1.6 0.9 %copy-done.1 = bf16[32,2048]{1,0:T(8,128)(2,1)S(1)} copy-done((bf16[32,2048]{1,0:T(8,128)(2,1)S(1)}, bf16[32,2048]{1,0:T(8,128)(2,1)}, u32[]{:S(2)}) %copy-start.1) | copy-done | bytes 131096
  2.5 0.0 copy-start.2
  2.5 0.7 %copy-done.2 = s32[2048]{0:T(1024)S(1)} copy-done((s32[2048]{0:T(1024)S(1)}, s32[2048]{0:T(1024)}, u32[]{:S(2)}) %copy-start.2) | copy-done | bytes 8216
  3.2 0.0 copy-start.3
  3.2 0.7 %copy-done.3 = s32[2,256]{1,0:T(2,128)S(1)} copy-done((s32[2,256]{1,0:T(2,128)S(1)}, s32[2,256]{1,0:T(2,128)}, u32[]{:S(2)}) %copy-start.3) | copy-done | bytes 2072
  3.9 30.5 %shard_map.64 = f32[32,1024]{1,0:T(8,128)S(1)} custom-call(bf16[64,2048]{1,0:T(8,128)(2,1)S(1)} %copy-done, bf16[32,2048]{1,0:T(8,128)(2,1)S(1)} %copy-done.1, s32[1,2048]{1,0:T(1,128)S(1)} %bitcast.3, s32[1,2]{1,0:T(1,128)S(1)} %copy-done.5, s32[1,256]{1,0:T(1,128)S(1)} %copy-done.4, s32[2,256]{1,0:T(2,128)S(1)} %copy-done.3), custom_call_target="tpu_custom_call" | custom-call | tf_op jit(solution)/shard_map/pallas_call | solution.py:260
  34.4 0.8 %copy.7 = f32[32,1,1024]{2,1,0:T(1,128)} copy(f32[32,1,1024]{2,0,1:T(8,128)S(1)} %bitcast.2) | data formatting | bytes 262144 | tf_op jit(solution)/shard_map/reshape | solution.py:284
Async XLA Ops:
  0.0 0.7 %copy-start.4 = (s32[1,256]{1,0:T(1,128)S(1)}, s32[1,256]{1,0:T(1,128)}, u32[]{:S(2)}) copy-start(s32[1,256]{1,0:T(1,128)} %skel.1) | copy-start | bytes 3076
  0.0 0.7 %copy-start.5 = (s32[1,2]{1,0:T(1,128)S(1)}, s32[1,2]{1,0:T(1,128)}, u32[]{:S(2)}) copy-start(s32[1,2]{1,0:T(1,128)} %mask.1) | copy-start | bytes 28
  0.7 1.0 %copy-start = (bf16[64,2048]{1,0:T(8,128)(2,1)S(1)}, bf16[64,2048]{1,0:T(8,128)(2,1)}, u32[]{:S(2)}) copy-start(bf16[64,2048]{1,0:T(8,128)(2,1)} %coords.1) | copy-start | bytes 786436
  1.6 0.9 %copy-start.1 = (bf16[32,2048]{1,0:T(8,128)(2,1)S(1)}, bf16[32,2048]{1,0:T(8,128)(2,1)}, u32[]{:S(2)}) copy-start(bf16[32,2048]{1,0:T(8,128)(2,1)} %values.1) | copy-start | bytes 393220
  2.5 0.7 %copy-start.2 = (s32[2048]{0:T(1024)S(1)}, s32[2048]{0:T(1024)}, u32[]{:S(2)}) copy-start(s32[2048]{0:T(1024)} %param.8) | copy-start | bytes 24580
  3.2 0.7 %copy-start.3 = (s32[2,256]{1,0:T(2,128)S(1)}, s32[2,256]{1,0:T(2,128)}, u32[]{:S(2)}) copy-start(s32[2,256]{1,0:T(2,128)} %skel_up.1) | copy-start | bytes 6148
where the time goes:
time: 35.4 us; the launch traced here: 35.2 us
  Pallas kernels  30.5 us (86%)
  local copies, waits for them, and re-layouts  4.7 us (13%)
    pallas_call x1, Pallas kernels, shards(): pl.pallas_call(functools.partial(body, (mesh.shape['blk'], sub_size)), ou...  30.5 us
    unnamed x12, local copies, waits for them, and re-layouts  3.91 us
    reshape x1, local copies, waits for them, and re-layouts, shards(): return result[:columns].reshape(columns, 1, half)  0.79 us

commit v1 on v0

--- a/solution.py
+++ b/solution.py
@@ -9,7 +9,7 @@
 
 MESH = pl.DeviceIdType.MESH
 DEPTH = 128
-CHUNK = 256
+TARGETS = 512
 
 
 def norm_rows(x, is_source, features):
@@ -46,6 +46,13 @@
 
 def body(
     sizes,
+    coords_hbm,
+    values_hbm,
+    order_hbm,
+    mask_hbm,
+    skel_hbm,
+    skel_up_hbm,
+    result,
     coords,
     values,
     order,
@@ -66,6 +73,7 @@
     f_recv,
     p_send,
     p_recv,
+    local_sems,
 ):
     blk_size, sub_size = sizes
     features, rows = coords.shape
@@ -77,6 +85,10 @@
     rhs = lax.axis_index("rhs")
     sub = lax.axis_index("sub")
 
+    def start_all(copies):
+        for copy in copies:
+            copy.start()
+
     def flip(number, bit):
         return number + bit - 2 * bit * ((number // bit) % 2)
 
@@ -87,9 +99,23 @@
     partners = [near_1, near_2] + chip_mates
     partners += [{"blk": flip(blk, 2**bit)} for bit in range(2, bits)]
 
+    loads = [
+        pltpu.make_async_copy(source, target, local_sems.at[place])
+        for place, (source, target) in enumerate(
+            [
+                (order_hbm, order),
+                (skel_hbm, skel),
+                (coords_hbm, coords),
+                (values_hbm, values),
+                (skel_up_hbm, skel_up),
+                (mask_hbm, mask),
+            ]
+        )
+    ]
     barrier = pltpu.get_barrier_semaphore()
     for partner in partners:
         pl.semaphore_signal(barrier, inc=1, device_id=partner, device_id_type=MESH)
+    start_all(loads)
     pl.semaphore_wait(barrier, len(partners))
 
     share = features // 4
@@ -114,7 +140,7 @@
             ),
         ]
 
-    hops = [far_copies(0, coords, values, near_1), far_copies(1, coords, values, near_2)]
+    hops = [far_copies(0, coords_hbm, values_hbm, near_1), far_copies(1, coords_hbm, values_hbm, near_2)]
     hops.append(far_copies(2, xs.at[1], vs.at[1], near_1))
 
     def spread_copies(slot):
@@ -138,16 +164,15 @@
         for bit in range(bits)
     ]
 
-    def start(copies):
-        for copy in copies:
-            copy.start()
-
     def arrive(copies):
         for copy in copies:
             copy.wait_recv()
 
-    start(hops[0])
-    start(hops[1])
+    start_all(hops[1])
+    start_all(hops[0])
+
+    for load in loads:
+        load.wait()
 
     local = order[...] - blk * rows
     own = coords[...]
@@ -179,29 +204,26 @@
     tgt[...] = augmented(gathered(pieces, mine), False)
 
     arrive(hops[0])
-    start(spreads[0])
+    start_all(spreads[0])
 
     out[...] = jnp.zeros_like(out)
 
     def near(slot, weights):
-        def step(index, carry):
-            at = pl.ds(pl.multiple_of(index * CHUNK, CHUNK), CHUNK)
-            tile = jnp.exp(dot(src_t[slot, at], tgt[...])).astype(jnp.bfloat16)
-            out[...] += dot(weights[:, at], tile)
-            return carry
-
-        lax.fori_loop(0, rows // CHUNK, step, 0)
+        for first in range(0, half, TARGETS):
+            at = pl.ds(first, TARGETS)
+            tile = jnp.exp(dot(src_t[slot], tgt[:, at])).astype(jnp.bfloat16)
+            out[:, at] += dot(weights[...], tile)
 
     near(0, values)
 
     arrive(hops[1])
-    start(hops[2])
-    start(spreads[1])
+    start_all(hops[2])
+    start_all(spreads[1])
 
     def near_slot(slot, column):
         arrive(spreads[slot])
         src_t[slot + 1] = augmented(xs[slot], True).T
-        factor = mask[0, column].astype(jnp.float32)
+        factor = mask[0:1, column : column + 1].astype(jnp.float32)
         scaled[slot] = (vs[slot].astype(jnp.float32) * factor).astype(jnp.bfloat16)
         near(slot + 1, scaled.at[slot])
 
@@ -227,7 +249,7 @@
     near_slot(0, 0)
     merge(0)
     arrive(hops[2])
-    start(spreads[2])
+    start_all(spreads[2])
     near_slot(1, 1)
     for bit in range(1, bits - 1):
         merge(bit)
@@ -236,14 +258,17 @@
     for bit in range(bits):
         weights = sibs[bit, features:]
         if bit < 2:
-            factor = (1 - mask[0, bit]).astype(jnp.float32)
+            factor = (1 - mask[0:1, bit : bit + 1]).astype(jnp.float32)
             weights = (weights.astype(jnp.float32) * factor).astype(jnp.bfloat16)
         tile = jnp.exp(dot(augmented(sibs[bit, :features], True).T, tgt[...])).astype(jnp.bfloat16)
         out[...] += dot(weights, tile)
 
+    store = pltpu.make_async_copy(out.at[: result.shape[0]], result.at[:, 0], local_sems.at[6])
+    store.start()
     for copies in hops + spreads + [pack_copies]:
         for copy in copies:
             copy.wait_send()
+    store.wait()
 
 
 def shards(mesh, coords, values, tree_order, near_mask, skel_leaf, skel_up):
@@ -256,13 +281,20 @@
     held = max(columns, 16)
     if held > columns:
         values = jnp.pad(values, ((0, held - columns), (0, 0)))
-    vmem = pl.BlockSpec(memory_space=pltpu.VMEM)
-    result = pl.pallas_call(
+    hbm = pl.BlockSpec(memory_space=pltpu.HBM)
+    return pl.pallas_call(
         functools.partial(body, (mesh.shape["blk"], sub_size)),
-        out_shape=jax.ShapeDtypeStruct((held, half), jnp.float32),
-        in_specs=[vmem, vmem, vmem, pl.BlockSpec(memory_space=pltpu.SMEM), vmem, vmem],
-        out_specs=vmem,
+        out_shape=jax.ShapeDtypeStruct((columns, 1, half), jnp.float32),
+        in_specs=[hbm] * 6,
+        out_specs=hbm,
         scratch_shapes=[
+            pltpu.VMEM((features, rows), jnp.bfloat16),
+            pltpu.VMEM((held, rows), jnp.bfloat16),
+            pltpu.VMEM((1, rows), jnp.int32),
+            pltpu.VMEM((1, 2), jnp.int32),
+            pltpu.VMEM((1, skeleton), jnp.int32),
+            pltpu.VMEM(skel_up.shape, jnp.int32),
+            pltpu.VMEM((held, half), jnp.float32),
             pltpu.VMEM((3, features, rows), jnp.bfloat16),
             pltpu.VMEM((3, held, rows), jnp.bfloat16),
             pltpu.VMEM((bits, features + held, skeleton), jnp.bfloat16),
@@ -276,12 +308,12 @@
             pltpu.SemaphoreType.DMA((3, 4)),
             pltpu.SemaphoreType.DMA((bits,)),
             pltpu.SemaphoreType.DMA((bits,)),
+            pltpu.SemaphoreType.DMA((7,)),
         ],
         compiler_params=pltpu.CompilerParams(
-            collective_id=0, has_side_effects=True, vmem_limit_bytes=48 * 2**20
+            collective_id=0, has_side_effects=True, vmem_limit_bytes=60 * 2**20
         ),
     )(coords, values, tree_order.reshape(1, rows), near_mask, skel_leaf, skel_up)
-    return result[:columns].reshape(columns, 1, half)
 
 
 def solution(mesh):

time: 35.4 us -> 28.8 us (0.81)
  Pallas kernels: 30.5 us -> 27.1 us
  local copies, waits for them, and re-layouts: 4.7 us -> 1.57 us
    pallas_call x1, Pallas kernels: 30.5 us -> 27.1 us  [shards(): pl.pallas_call(functools.partial(body, (mesh.shape['blk'], sub_size)), ou...]
    unnamed x12 -> x1, local copies, waits for them, and re-layouts: 3.91 us -> 1.57 us
    reshape x1 -> x0, local copies, waits for them, and re-layouts: 0.79 us -> none  [shards(): return result[:columns].reshape(columns, 1, half)]
where the time goes in v1:
time: 28.8 us; the launch traced here: 28.7 us
  Pallas kernels  27.1 us (94%)
  local copies, waits for them, and re-layouts  1.57 us (5%)
    pallas_call x1, Pallas kernels, shards(): pl.pallas_call(functools.partial(body, (mesh.shape['blk'], sub_size)), ou...  27.1 us
    unnamed x1, local copies, waits for them, and re-layouts  1.57 us

profile of v1, /device:TPU:0, one launch (start us, length us, event | category | flops | bytes accessed | tf_op | source)
XLA Modules:
  0.0 28.7 jit_solution(3405209775096648694)
XLA Ops:
  0.0 27.1 %shard_map.64 = f32[32,1,1024]{2,1,0:T(1,128)} custom-call(bf16[64,2048]{1,0:T(8,128)(2,1)} %coords_hbm.1, bf16[32,2048]{1,0:T(8,128)(2,1)} %values_hbm.1, s32[1,2048]{1,0:T(1,128)} %bitcast.1, s32[1,2]{1,0:T(1,128)} %mask_hbm.1, s32[1,256]{1,0:T(1,128)} %skel_hbm.1, s32[2,256]{1,0:T(2,128)} %skel_up_hbm.1), custom_call_target="tpu_custom_call" | custom-call | tf_op jit(solution)/shard_map/pallas_call | solution.py:285
  27.1 1.6 %copy.8 = f32[32,1,1024]{2,1,0:T(1,128)} copy(f32[32,1,1024]{2,1,0:T(1,128)} %shard_map.64) | data formatting | bytes 262144
